TPU v7x, 128 devices: a whole 4x4x4 slice. The times are simulated.
128 devices in a mesh: cp: 64 (over x, y, z), hd: 2 (over core).
Axes of the slice: x: 4, y: 4, z: 4, core: 2. Of those that a mesh axis runs over, the one named last changes fastest.
Arguments:
- doc_lengths: int32 [16], replicated, may hold values from 1 to 1792, 16384 in all
- queries: bfloat16 [16384, 4096], P(('cp', 'hd')), may hold values from -6 to 6, as said below
- keys: bfloat16 [16384, 1024], P(('cp', 'hd')), may hold values from -6 to 6, as said below
- values: bfloat16 [16384, 1024], P(('cp', 'hd')), may hold values from -6 to 6
- output_gradient: bfloat16 [16384, 4096], P(('cp', 'hd')), may hold values from -6 to 6
Outputs:
- attended: bfloat16 [16384, 4096], P(('cp', 'hd'))
- grad_queries: bfloat16 [16384, 4096], P(('cp', 'hd'))
- grad_keys: bfloat16 [16384, 1024], P(('cp', 'hd'))
- grad_values: bfloat16 [16384, 1024], P(('cp', 'hd'))
Inputs may be any that keep to these rules, and one draw needn't show every extreme that they name: `doc_lengths`: documents lie end to end and sum to 16384 tokens; the longest has exactly 1792. `queries`: entries of order one. `keys`: entries of order one.
All inputs are finite; a program needn't handle non-finite values.
Results may differ from a plain program's by a relative error of at most 0.012.
The roundings to bfloat16 on the way count: a program that leaves them out, or rounds other values in their place, can miss the bound.
Values may be sent and summed in bfloat16 or wider, within the bound.
No kernel may reach another device: no remote copies, remote signals or barrier semaphores. Data moves between devices by JAX's collectives and lax.ppermute only.
A program may use at most 128 MiB of HBM per device.

v0:
```python
import jax
import jax.numpy as jnp
from jax import lax
from jax.experimental import pallas as pl
from jax.experimental.pallas import tpu as pltpu
from jax.sharding import Mesh, PartitionSpec as P

HEAD = 128
GROUP = 4
BLOCK = 256
STEP = 1024
ROW = 1024
BEHIND = 1792
WINDOW = BEHIND + ROW
TILES = ROW // BLOCK
WIDE = GROUP * BLOCK
SCALE = HEAD ** (-0.5)
LOG2E = 1.4426950408889634
AXES = ("x", "y", "z", "hd")
ROWS = ("z", "hd")

NT = (((1,), (1,)), ((), ()))
TN = (((0,), (0,)), ((), ()))
NN = (((1,), (0,)), ((), ()))


def dot(a, b, dims):
    return lax.dot_general(a, b, dims, preferred_element_type=jnp.float32)


def attention_kernel(
    doc_ref, qg_ref, kv2_ref, kv1_ref, kv0_ref, out_ref, d2_ref, d1_ref, d0_ref, kv, acc, scores, oacc, qacc, top, sums
):
    tile = pl.program_id(0)
    row = lax.axis_index("x") * 4 + lax.axis_index("y")

    @pl.when(tile == 0)
    def _():
        kv[0:768] = kv2_ref[...]
        kv[768:1792] = kv1_ref[...]
        kv[1792:2816] = kv0_ref[...]
        acc[...] = jnp.zeros_like(acc)

    origin = row * ROW - BEHIND
    first_query = BEHIND + tile * BLOCK
    query_at = first_query + lax.broadcasted_iota(jnp.int32, (1, BLOCK), 1)
    start_at = jnp.full((1, BLOCK), -origin, jnp.int32)
    first_start = -origin
    end = -origin
    for n in range(16):
        end = end + doc_ref[n]
        start_at = jnp.where(query_at >= end, end, start_at)
        first_start = jnp.where(first_query >= end, end, first_start)
    low = first_start // BLOCK * BLOCK
    span = first_query + BLOCK - low
    steps = span // STEP
    rest = span - steps * STEP

    def sweep(step):
        def whole(n, _):
            step(pl.multiple_of(n * STEP, STEP), STEP)
            return 0

        lax.fori_loop(0, steps, whole, 0)
        for size in range(BLOCK, STEP, BLOCK):

            @pl.when(rest == size)
            def _():
                step(pl.multiple_of(steps * STEP, STEP), size)

    def keys_at(off, size):
        return pl.ds(pl.multiple_of(low + off, BLOCK), size)

    qg = qg_ref[...].reshape(BLOCK, 2 * GROUP * HEAD)
    q = jnp.concatenate([qg[:, h * HEAD : (h + 1) * HEAD] for h in range(GROUP)], axis=0)
    g = jnp.concatenate([qg[:, (GROUP + h) * HEAD : (GROUP + h + 1) * HEAD] for h in range(GROUP)], axis=0)

    top[...] = jnp.full_like(top, -jnp.inf)
    sums[...] = jnp.zeros_like(sums)
    oacc[...] = jnp.zeros_like(oacc)
    qacc[...] = jnp.zeros_like(qacc)

    def score_step(off, size):
        s = dot(kv[keys_at(off, size), :HEAD], q, NT)
        key_at = low + off + lax.broadcasted_iota(jnp.int32, (size, BLOCK), 0)
        allowed = (key_at >= start_at) & (key_at <= query_at)
        s = jnp.where(jnp.concatenate([allowed] * GROUP, axis=1), s, -jnp.inf)
        scores[pl.ds(off, size)] = s
        top[...] = jnp.maximum(top[...], jnp.max(s.reshape(size // 8, 8, WIDE), axis=0))

    sweep(score_step)
    peak = jnp.max(top[...], axis=0, keepdims=True)

    def exp_step(off, size):
        e = jnp.exp2((scores[pl.ds(off, size)] - peak) * (SCALE * LOG2E))
        scores[pl.ds(off, size)] = e
        sums[...] += jnp.sum(e.reshape(size // 8, 8, WIDE), axis=0)

    sweep(exp_step)
    inverse = 1.0 / jnp.sum(sums[...], axis=0, keepdims=True)

    def out_step(off, size):
        at = keys_at(off, size)
        p = (scores[pl.ds(off, size)] * inverse).astype(jnp.bfloat16)
        oacc[...] += dot(kv[at, HEAD:], p, TN)
        acc[at, HEAD:] += dot(p, g, NN)

    sweep(out_step)
    attended = oacc[...].astype(jnp.bfloat16)
    delta = jnp.sum(attended.astype(jnp.float32) * g.T.astype(jnp.float32), axis=0, keepdims=True)
    attended = attended.T
    inverse = inverse * SCALE

    def grad_step(off, size):
        at = keys_at(off, size)
        dp = dot(kv[at, HEAD:], g, NT)
        ds = (scores[pl.ds(off, size)] * inverse * (dp - delta)).astype(jnp.bfloat16)
        qacc[...] += dot(kv[at, :HEAD], ds, TN)
        acc[at, :HEAD] += dot(ds, q, NN)

    sweep(grad_step)
    grad_q = qacc[...].astype(jnp.bfloat16).T
    for h in range(GROUP):
        for half in range(BLOCK // 128):
            rows = slice(h * BLOCK + half * 128, h * BLOCK + half * 128 + 128)
            out_ref[half, :, h * HEAD : (h + 1) * HEAD] = attended[rows]
            out_ref[half, :, (GROUP + h) * HEAD : (GROUP + h + 1) * HEAD] = grad_q[rows]

    @pl.when(tile == TILES - 1)
    def _():
        d2_ref[...] = acc[0:768].astype(jnp.bfloat16)
        d1_ref[...] = acc[768:1792].astype(jnp.bfloat16)
        d0_ref[...] = acc[1792:2816]


def attention(doc_lengths, qg, kv2, kv1, kv0):
    whole = lambda *shape: pl.BlockSpec(shape, lambda i: (0,) * len(shape))
    tiled = pl.BlockSpec((2, 128, 2 * GROUP * HEAD), lambda i: (i, 0, 0))
    return pl.pallas_call(
        attention_kernel,
        grid=(TILES,),
        in_specs=[
            pl.BlockSpec(memory_space=pltpu.SMEM),
            tiled,
            whole(768, 256),
            whole(1024, 256),
            whole(1024, 256),
        ],
        out_specs=[tiled, whole(768, 256), whole(1024, 256), whole(1024, 256)],
        out_shape=[
            jax.ShapeDtypeStruct((8, 128, 2 * GROUP * HEAD), jnp.bfloat16),
            jax.ShapeDtypeStruct((768, 256), jnp.bfloat16),
            jax.ShapeDtypeStruct((1024, 256), jnp.bfloat16),
            jax.ShapeDtypeStruct((1024, 256), jnp.float32),
        ],
        scratch_shapes=[
            pltpu.VMEM((WINDOW, 256), jnp.bfloat16),
            pltpu.VMEM((WINDOW, 256), jnp.float32),
            pltpu.VMEM((BEHIND + BLOCK, WIDE), jnp.float32),
            pltpu.VMEM((HEAD, WIDE), jnp.float32),
            pltpu.VMEM((HEAD, WIDE), jnp.float32),
            pltpu.VMEM((8, WIDE), jnp.float32),
            pltpu.VMEM((8, WIDE), jnp.float32),
        ],
        compiler_params=pltpu.CompilerParams(vmem_limit_bytes=48 * 1024 * 1024),
        name="attention",
    )(doc_lengths, qg, kv2, kv1, kv0)


def shift(x, by):
    pairs = [(i, i + by) for i in range(64) if 0 <= i + by < 64]
    return lax.ppermute(x, ("x", "y", "z"), pairs)


def swap(x):
    return lax.all_to_all(x, ROWS, split_axis=0, concat_axis=0, tiled=False)


def pack_kernel(a_ref, b_ref, out_ref):
    groups, _, width = out_ref.shape
    for n in range(groups):
        columns = slice(n * (width // 2), (n + 1) * (width // 2))
        out_ref[n, :, : width // 2] = a_ref[:, columns]
        out_ref[n, :, width // 2 :] = b_ref[:, columns]


def pack(a, b, steps):
    tokens, width = a.shape
    return pl.pallas_call(
        pack_kernel,
        grid=(steps,),
        in_specs=[pl.BlockSpec((tokens, width // steps), lambda i: (0, i))] * 2,
        out_specs=pl.BlockSpec((8 // steps, tokens, width // 4), lambda i: (i, 0, 0)),
        out_shape=jax.ShapeDtypeStruct((8, tokens, width // 4), a.dtype),
        name="pack",
    )(a, b)


def unpack_kernel(x_ref, a_ref, b_ref):
    groups, _, width = x_ref.shape
    for n in range(groups):
        columns = slice(n * (width // 2), (n + 1) * (width // 2))
        a_ref[:, columns] = x_ref[n, :, : width // 2]
        b_ref[:, columns] = x_ref[n, :, width // 2 :]


def unpack(x, steps, limit=None):
    _, tokens, half = x.shape
    width = half * 4
    return pl.pallas_call(
        unpack_kernel,
        grid=(steps,),
        in_specs=[pl.BlockSpec((8 // steps, tokens, half), lambda i: (i, 0, 0))],
        out_specs=[pl.BlockSpec((tokens, width // steps), lambda i: (0, i))] * 2,
        out_shape=[jax.ShapeDtypeStruct((tokens, width), x.dtype)] * 2,
        compiler_params=pltpu.CompilerParams(vmem_limit_bytes=limit),
        name="unpack",
    )(x)


def body(doc_lengths, queries, keys, values, output_gradient):
    kv0 = swap(pack(keys, values, 1)).reshape(ROW, 256)
    kv1 = shift(kv0, 4)
    kv2 = shift(kv0[256:], 8)
    qg = swap(pack(queries, output_gradient, 4))
    out, d2, d1, d0 = attention(doc_lengths, qg, kv2, kv1, kv0)
    d1 = shift(d1, -4).astype(jnp.float32)
    d2 = shift(d2, -8).astype(jnp.float32)
    total = d0 + d1 + jnp.pad(d2, ((256, 0), (0, 0)))
    total, out = lax.optimization_barrier((total.astype(jnp.bfloat16), swap(out)))
    grad_keys, grad_values = unpack(swap(total.reshape(8, 128, 256)), 1, 8 * 1024 * 1024)
    attended, grad_queries = unpack(out, 4)
    return attended, grad_queries, grad_keys, grad_values


def solution(mesh):
    grid = Mesh(mesh.devices.reshape(4, 4, 4, 2), AXES)
    tokens = P(AXES, None)
    return jax.shard_map(
        body,
        mesh=grid,
        in_specs=(P(None), tokens, tokens, tokens, tokens),
        out_specs=(tokens, tokens, tokens, tokens),
        check_vma=False,
    )
```

profile of v0, /device:TPU:20, one launch (start us, length us, event | category | flops | bytes accessed | tf_op | source)
XLA Modules:
  0.0 133.6 jit_solution(1157498731401922266)
XLA Ops:
  0.6 1.9 %pack.3 = bf16[8,128,256]{2,1,0:T(8,128)(2,1)} custom-call(bf16[128,1024]{1,0:T(8,128)(2,1)} %a_ref.3, bf16[128,1024]{1,0:T(8,128)(2,1)} %b_ref.3), custom_call_target="tpu_custom_call" | custom-call | tf_op jit(solution)/shard_map/pack/pallas_call | solution.py:189
  2.5 5.3 %all-to-all-start.1 = ((bf16[8,128,256]{2,1,0:T(8,128)(2,1)}), bf16[8,128,256]{2,1,0:T(8,128)(2,1)S(1)}, u32[]{:S(2)}, u32[]{:S(2)}) async-start(bf16[8,128,256]{2,1,0:T(8,128)(2,1)} %pack.3), calls=%async_computation.1 | async-start | bytes 1048576 | tf_op jit(solution)/shard_map/all_to_all | solution.py:176
  7.9 3.8 %pack.2 = bf16[8,128,1024]{2,1,0:T(8,128)(2,1)} custom-call(bf16[128,4096]{1,0:T(8,128)(2,1)} %a_ref.2, bf16[128,4096]{1,0:T(8,128)(2,1)} %b_ref.2), custom_call_target="tpu_custom_call" | custom-call | tf_op jit(solution)/shard_map/pack/pallas_call | solution.py:189
  11.6 0.0 copy-start
  11.6 6.6 %all-to-all-done.1 = bf16[8,128,256]{2,1,0:T(8,128)(2,1)S(1)} async-done(((bf16[8,128,256]{2,1,0:T(8,128)(2,1)}), bf16[8,128,256]{2,1,0:T(8,128)(2,1)S(1)}, u32[]{:S(2)}, u32[]{:S(2)}) %all-to-all-start.1) | async-done | bytes 524320 | tf_op jit(solution)/shard_map/all_to_all | solution.py:176
  18.2 4.3 %all-to-all-start = ((bf16[8,128,1024]{2,1,0:T(8,128)(2,1)}), bf16[8,128,1024]{2,1,0:T(8,128)(2,1)}, u32[]{:S(2)}, u32[]{:S(2)}) async-start(bf16[8,128,1024]{2,1,0:T(8,128)(2,1)} %pack.2), calls=%async_computation | async-start | bytes 4194304 | tf_op jit(solution)/shard_map/all_to_all | solution.py:176
  22.6 3.2 %collective-permute-start.1 = (bf16[1024,256]{1,0:T(8,128)(2,1)S(1)}, bf16[1024,256]{1,0:T(8,128)(2,1)S(1)}, u32[]{:S(2)}, u32[]{:S(2)}) collective-permute-start(bf16[1024,256]{1,0:T(8,128)(2,1)S(1)} %bitcast.3), channel_id=1, source_target_pairs={{0,8},{2,10},{4,12},{6,14},{8,16},{10,18},{12,20},{14,22},{16,24},... | collective-permute-start | bytes 1572872 | tf_op jit(solution)/shard_map/ppermute | solution.py:172
  25.8 3.2 %collective-permute-start = (bf16[768,256]{1,0:T(8,128)(2,1)S(1)}, bf16[768,256]{1,0:T(8,128)(2,1)S(1)}, u32[]{:S(2)}, u32[]{:S(2)}) collective-permute-start(bf16[768,256]{1,0:T(8,128)(2,1)S(1)} %bitcast.5), channel_id=1, source_target_pairs={{0,16},{2,18},{4,20},{6,22},{8,24},{10,26},{12,28},{14,30},{16,32}... | collective-permute-start | bytes 1179656 | tf_op jit(solution)/shard_map/ppermute | solution.py:172
  29.0 18.1 %collective-permute-done.kv2_ref = bf16[768,256]{1,0:T(8,128)(2,1)S(1)} collective-permute-done((bf16[768,256]{1,0:T(8,128)(2,1)S(1)}, bf16[768,256]{1,0:T(8,128)(2,1)S(1)}, u32[]{:S(2)}, u32[]{:S(2)}) %collective-permute-start) | collective-permute-done | bytes 393248 | tf_op jit(solution)/shard_map/ppermute | solution.py:172
  47.1 0.0 collective-permute-done.1.kv1_ref
  47.1 2.7 %all-to-all-done.qg_ref = bf16[8,128,1024]{2,1,0:T(8,128)(2,1)} async-done(((bf16[8,128,1024]{2,1,0:T(8,128)(2,1)}), bf16[8,128,1024]{2,1,0:T(8,128)(2,1)}, u32[]{:S(2)}, u32[]{:S(2)}) %all-to-all-start) | async-done | bytes 2097184 | tf_op jit(solution)/shard_map/all_to_all | solution.py:176
  49.8 0.0 copy-done
  49.8 16.8 %attention.1 = (bf16[8,128,1024]{2,1,0:T(8,128)(2,1)}, bf16[768,256]{1,0:T(8,128)(2,1)S(1)}, bf16[1024,256]{1,0:T(8,128)(2,1)S(1)}, f32[1024,256]{1,0:T(8,128)S(1)}) custom-call(s32[16]{0:T(128)S(1)} %copy-done, bf16[8,128,1024]{2,1,0:T(8,128)(2,1)} %all-to-all-done.qg_ref, bf16[768,256]{1,0:T(8,128)(2,1)S(1)} %collective-permute-done.kv2_ref, ...), custom_call_target="tpu_custom_call" | custom-call | tf_op jit(solution)/shard_map/attention/pallas_call | solution.py:139
  66.6 4.3 %all-to-all-start.2 = ((bf16[8,128,1024]{2,1,0:T(8,128)(2,1)}), bf16[8,128,1024]{2,1,0:T(8,128)(2,1)}, u32[]{:S(2)}, u32[]{:S(2)}) async-start(bf16[8,128,1024]{2,1,0:T(8,128)(2,1)} %get-tuple-element.17), calls=%async_computation.2 | async-start | bytes 4194304 | tf_op jit(solution)/shard_map/all_to_all | solution.py:176
  70.9 19.5 %collective-permute-start.2 = (bf16[1024,256]{1,0:T(8,128)(2,1)S(1)}, bf16[1024,256]{1,0:T(8,128)(2,1)S(1)}, u32[]{:S(2)}, u32[]{:S(2)}) collective-permute-start(bf16[1024,256]{1,0:T(8,128)(2,1)S(1)} %get-tuple-element.15), channel_id=1, source_target_pairs={{8,0},{10,2},{12,4},{14,6},{16,8},{18,10},{20,12},{22,14},{24,16},... | collective-permute-start | bytes 1572872 | tf_op jit(solution)/shard_map/ppermute | solution.py:172
  90.5 1.9 %collective-permute-start.3 = (bf16[768,256]{1,0:T(8,128)(2,1)S(1)}, bf16[768,256]{1,0:T(8,128)(2,1)S(1)}, u32[]{:S(2)}, u32[]{:S(2)}) collective-permute-start(bf16[768,256]{1,0:T(8,128)(2,1)S(1)} %get-tuple-element.16), channel_id=1, source_target_pairs={{16,0},{18,2},{20,4},{22,6},{24,8},{26,10},{28,12},{30,14},{32,16}... | collective-permute-start | bytes 1179656 | tf_op jit(solution)/shard_map/ppermute | solution.py:172
  92.4 24.7 %collective-permute-done.3 = bf16[768,256]{1,0:T(8,128)(2,1)S(1)} collective-permute-done((bf16[768,256]{1,0:T(8,128)(2,1)S(1)}, bf16[768,256]{1,0:T(8,128)(2,1)S(1)}, u32[]{:S(2)}, u32[]{:S(2)}) %collective-permute-start.3) | collective-permute-done | bytes 393248 | tf_op jit(solution)/shard_map/ppermute | solution.py:172
  117.1 0.0 collective-permute-done.2
  117.1 0.9 add_convert_fusion
  118.0 0.0 all-to-all-done.2.x_ref
  118.0 4.3 %all-to-all-start.3 = ((bf16[8,128,256]{2,1,0:T(8,128)(2,1)}), bf16[8,128,256]{2,1,0:T(8,128)(2,1)S(1)}, u32[]{:S(2)}, u32[]{:S(2)}) async-start(bf16[8,128,256]{2,1,0:T(8,128)(2,1)} %bitcast.2), calls=%async_computation.3 | async-start | bytes 1048576 | tf_op jit(solution)/shard_map/all_to_all | solution.py:176
  122.3 3.8 %unpack.2 = (bf16[128,4096]{1,0:T(8,128)(2,1)}, bf16[128,4096]{1,0:T(8,128)(2,1)}) custom-call(bf16[8,128,1024]{2,1,0:T(8,128)(2,1)} %all-to-all-done.2.x_ref), custom_call_target="tpu_custom_call" | custom-call | tf_op jit(solution)/shard_map/unpack/pallas_call | solution.py:210
  126.1 6.6 %all-to-all-done.3.x_ref = bf16[8,128,256]{2,1,0:T(8,128)(2,1)S(1)} async-done(((bf16[8,128,256]{2,1,0:T(8,128)(2,1)}), bf16[8,128,256]{2,1,0:T(8,128)(2,1)S(1)}, u32[]{:S(2)}, u32[]{:S(2)}) %all-to-all-start.3) | async-done | bytes 524320 | tf_op jit(solution)/shard_map/all_to_all | solution.py:176
  132.7 0.9 unpack.3
  (1 shorter events, 0.0 us)
Async XLA Ops:
  2.5 15.7 %all-to-all-start.1 = ((bf16[8,128,256]{2,1,0:T(8,128)(2,1)}), bf16[8,128,256]{2,1,0:T(8,128)(2,1)S(1)}, u32[]{:S(2)}, u32[]{:S(2)}) async-start(bf16[8,128,256]{2,1,0:T(8,128)(2,1)} %pack.3), calls=%async_computation.1 | async-start | bytes 1048576 | tf_op jit(solution)/shard_map/all_to_all | solution.py:176
  11.6 38.1 %copy-start = (s32[16]{0:T(128)S(1)}, s32[16]{0:T(128)}, u32[]{:S(2)}) copy-start(s32[16]{0:T(128)} %doc_ref.1) | copy-start | bytes 196
  18.2 31.6 %all-to-all-start = ((bf16[8,128,1024]{2,1,0:T(8,128)(2,1)}), bf16[8,128,1024]{2,1,0:T(8,128)(2,1)}, u32[]{:S(2)}, u32[]{:S(2)}) async-start(bf16[8,128,1024]{2,1,0:T(8,128)(2,1)} %pack.2), calls=%async_computation | async-start | bytes 4194304 | tf_op jit(solution)/shard_map/all_to_all | solution.py:176
  22.6 24.5 %collective-permute-start.1 = (bf16[1024,256]{1,0:T(8,128)(2,1)S(1)}, bf16[1024,256]{1,0:T(8,128)(2,1)S(1)}, u32[]{:S(2)}, u32[]{:S(2)}) collective-permute-start(bf16[1024,256]{1,0:T(8,128)(2,1)S(1)} %bitcast.3), channel_id=1, source_target_pairs={{0,8},{2,10},{4,12},{6,14},{8,16},{10,18},{12,20},{14,22},{16,24},... | collective-permute-start | bytes 1572872 | tf_op jit(solution)/shard_map/ppermute | solution.py:172
  25.8 21.3 %collective-permute-start = (bf16[768,256]{1,0:T(8,128)(2,1)S(1)}, bf16[768,256]{1,0:T(8,128)(2,1)S(1)}, u32[]{:S(2)}, u32[]{:S(2)}) collective-permute-start(bf16[768,256]{1,0:T(8,128)(2,1)S(1)} %bitcast.5), channel_id=1, source_target_pairs={{0,16},{2,18},{4,20},{6,22},{8,24},{10,26},{12,28},{14,30},{16,32}... | collective-permute-start | bytes 1179656 | tf_op jit(solution)/shard_map/ppermute | solution.py:172
  66.6 51.5 %all-to-all-start.2 = ((bf16[8,128,1024]{2,1,0:T(8,128)(2,1)}), bf16[8,128,1024]{2,1,0:T(8,128)(2,1)}, u32[]{:S(2)}, u32[]{:S(2)}) async-start(bf16[8,128,1024]{2,1,0:T(8,128)(2,1)} %get-tuple-element.17), calls=%async_computation.2 | async-start | bytes 4194304 | tf_op jit(solution)/shard_map/all_to_all | solution.py:176
  70.9 46.2 %collective-permute-start.2 = (bf16[1024,256]{1,0:T(8,128)(2,1)S(1)}, bf16[1024,256]{1,0:T(8,128)(2,1)S(1)}, u32[]{:S(2)}, u32[]{:S(2)}) collective-permute-start(bf16[1024,256]{1,0:T(8,128)(2,1)S(1)} %get-tuple-element.15), channel_id=1, source_target_pairs={{8,0},{10,2},{12,4},{14,6},{16,8},{18,10},{20,12},{22,14},{24,16},... | collective-permute-start | bytes 1572872 | tf_op jit(solution)/shard_map/ppermute | solution.py:172
  90.5 26.6 %collective-permute-start.3 = (bf16[768,256]{1,0:T(8,128)(2,1)S(1)}, bf16[768,256]{1,0:T(8,128)(2,1)S(1)}, u32[]{:S(2)}, u32[]{:S(2)}) collective-permute-start(bf16[768,256]{1,0:T(8,128)(2,1)S(1)} %get-tuple-element.16), channel_id=1, source_target_pairs={{16,0},{18,2},{20,4},{22,6},{24,8},{26,10},{28,12},{30,14},{32,16}... | collective-permute-start | bytes 1179656 | tf_op jit(solution)/shard_map/ppermute | solution.py:172
  118.0 14.7 %all-to-all-start.3 = ((bf16[8,128,256]{2,1,0:T(8,128)(2,1)}), bf16[8,128,256]{2,1,0:T(8,128)(2,1)S(1)}, u32[]{:S(2)}, u32[]{:S(2)}) async-start(bf16[8,128,256]{2,1,0:T(8,128)(2,1)} %bitcast.2), calls=%async_computation.3 | async-start | bytes 1048576 | tf_op jit(solution)/shard_map/all_to_all | solution.py:176
where the time goes:
time: 133 us; the launch traced here: 134 us
  waiting for transfers between devices  58.6 us (44%)
  starting transfers between devices  46.2 us (35%)
  Pallas kernels  27.2 us (20%)
    ppermute x4, waiting for transfers between devices, shift(): return lax.ppermute(x, ('x', 'y', 'z'), pairs)  42.8 us
    ppermute x4, starting transfers between devices, shift(): return lax.ppermute(x, ('x', 'y', 'z'), pairs)  27.8 us
    all_to_all x4, starting transfers between devices, swap(): return lax.all_to_all(x, ROWS, split_axis=0, concat_axis=0, tiled=False)  18.3 us
    pallas_call x1, Pallas kernels, attention(): pl.pallas_call(attention_kernel, grid=(TILES,), in_specs=[pl.BlockSpec(me...  16.8 us
    all_to_all x4, waiting for transfers between devices, swap(): return lax.all_to_all(x, ROWS, split_axis=0, concat_axis=0, tiled=False)  15.8 us
    pallas_call x2, Pallas kernels, pack(): pl.pallas_call(pack_kernel, grid=(steps,), in_specs=[pl.BlockSpec((tokens...  5.69 us
    pallas_call x2, Pallas kernels, unpack(): pl.pallas_call(unpack_kernel, grid=(steps,), in_specs=[pl.BlockSpec((8 //...  4.71 us
  transfers between devices with their start and end apart: 8, of which 5 were waited for; matrix products, arithmetic and copies ran while one was open for 1% of the time, Pallas kernels for 6%

commit v1 on v0

--- a/solution.py
+++ b/solution.py
@@ -172,6 +172,20 @@
     return lax.ppermute(x, ("x", "y", "z"), pairs)
 
 
+def between(i):
+    return i + 4 if i // 4 % 4 == 2 else i - 12
+
+
+def shift_two(x, back):
+    first = [(i, between(i)) for i in range(8, 64)]
+    second = [(between(i), i - 8) for i in range(8, 64)]
+    if not back:
+        first, second = [(b, a) for a, b in second], [(b, a) for a, b in first]
+    for pairs in (first, second):
+        x = lax.ppermute(x, ("x", "y", "z"), pairs)
+    return x
+
+
 def swap(x):
     return lax.all_to_all(x, ROWS, split_axis=0, concat_axis=0, tiled=False)
 
@@ -221,11 +235,11 @@
 def body(doc_lengths, queries, keys, values, output_gradient):
     kv0 = swap(pack(keys, values, 1)).reshape(ROW, 256)
     kv1 = shift(kv0, 4)
-    kv2 = shift(kv0[256:], 8)
+    kv2 = shift_two(kv0[256:], False)
     qg = swap(pack(queries, output_gradient, 4))
     out, d2, d1, d0 = attention(doc_lengths, qg, kv2, kv1, kv0)
     d1 = shift(d1, -4).astype(jnp.float32)
-    d2 = shift(d2, -8).astype(jnp.float32)
+    d2 = shift_two(d2, True).astype(jnp.float32)
     total = d0 + d1 + jnp.pad(d2, ((256, 0), (0, 0)))
     total, out = lax.optimization_barrier((total.astype(jnp.bfloat16), swap(out)))
     grad_keys, grad_values = unpack(swap(total.reshape(8, 128, 256)), 1, 8 * 1024 * 1024)

time: 133 us -> 127 us (0.955)
  the two profiles are of different devices: /device:TPU:20 before, /device:TPU:2 now
where the time goes in v1:
time: 127 us
  waiting for transfers between devices  52.2 us (41%)
  starting transfers between devices  46.2 us (36%)
  Pallas kernels  27.2 us (21%)
    ppermute x4, waiting for transfers between devices, shift_two(): x = lax.ppermute(x, ('x', 'y', 'z'), pairs)  34.2 us
    ppermute x4, starting transfers between devices, shift_two(): x = lax.ppermute(x, ('x', 'y', 'z'), pairs)  22.4 us
    all_to_all x4, starting transfers between devices, swap(): return lax.all_to_all(x, ROWS, split_axis=0, concat_axis=0, tiled=False)  18.2 us
    pallas_call x1, Pallas kernels, attention(): pl.pallas_call(attention_kernel, grid=(TILES,), in_specs=[pl.BlockSpec(me...  16.8 us
    all_to_all x4, waiting for transfers between devices, swap(): return lax.all_to_all(x, ROWS, split_axis=0, concat_axis=0, tiled=False)  13.1 us
    pallas_call x2, Pallas kernels, pack(): pl.pallas_call(pack_kernel, grid=(steps,), in_specs=[pl.BlockSpec((tokens...  5.7 us
    ppermute x2, starting transfers between devices, shift(): return lax.ppermute(x, ('x', 'y', 'z'), pairs)  5.55 us
    ppermute x2, waiting for transfers between devices, shift(): return lax.ppermute(x, ('x', 'y', 'z'), pairs)  4.86 us
  transfers between devices with their start and end apart: 10, of which 8 were waited for; matrix products, arithmetic and copies ran while one was open for 1% of the time, Pallas kernels for 6%

profile of v1, /device:TPU:2, one launch (start us, length us, event | category | flops | bytes accessed | tf_op | source)
XLA Modules:
  0.0 127.3 jit_solution(3228040079935791819)
XLA Ops:
  0.6 1.9 %pack.3 = bf16[8,128,256]{2,1,0:T(8,128)(2,1)} custom-call(bf16[128,1024]{1,0:T(8,128)(2,1)} %a_ref.3, bf16[128,1024]{1,0:T(8,128)(2,1)} %b_ref.3), custom_call_target="tpu_custom_call" | custom-call | tf_op jit(solution)/shard_map/pack/pallas_call | solution.py:203
  2.5 5.3 %all-to-all-start.1 = ((bf16[8,128,256]{2,1,0:T(8,128)(2,1)}), bf16[8,128,256]{2,1,0:T(8,128)(2,1)S(1)}, u32[]{:S(2)}, u32[]{:S(2)}) async-start(bf16[8,128,256]{2,1,0:T(8,128)(2,1)} %pack.3), calls=%async_computation.1 | async-start | bytes 1048576 | tf_op jit(solution)/shard_map/all_to_all | solution.py:190
  7.9 3.8 %pack.2 = bf16[8,128,1024]{2,1,0:T(8,128)(2,1)} custom-call(bf16[128,4096]{1,0:T(8,128)(2,1)} %a_ref.2, bf16[128,4096]{1,0:T(8,128)(2,1)} %b_ref.2), custom_call_target="tpu_custom_call" | custom-call | tf_op jit(solution)/shard_map/pack/pallas_call | solution.py:203
  11.6 6.6 %all-to-all-done.1 = bf16[8,128,256]{2,1,0:T(8,128)(2,1)S(1)} async-done(((bf16[8,128,256]{2,1,0:T(8,128)(2,1)}), bf16[8,128,256]{2,1,0:T(8,128)(2,1)S(1)}, u32[]{:S(2)}, u32[]{:S(2)}) %all-to-all-start.1) | async-done | bytes 524320 | tf_op jit(solution)/shard_map/all_to_all | solution.py:190
  18.2 4.4 %all-to-all-start = ((bf16[8,128,1024]{2,1,0:T(8,128)(2,1)}), bf16[8,128,1024]{2,1,0:T(8,128)(2,1)}, u32[]{:S(2)}, u32[]{:S(2)}) async-start(bf16[8,128,1024]{2,1,0:T(8,128)(2,1)} %pack.2), calls=%async_computation | async-start | bytes 4194304 | tf_op jit(solution)/shard_map/all_to_all | solution.py:190
  22.6 4.9 %collective-permute-start = (bf16[768,256]{1,0:T(8,128)(2,1)S(1)}, bf16[768,256]{1,0:T(8,128)(2,1)S(1)}, u32[]{:S(2)}, u32[]{:S(2)}) collective-permute-start(bf16[768,256]{1,0:T(8,128)(2,1)S(1)} %bitcast.5), channel_id=1, source_target_pairs={{0,24},{2,26},{4,28},{6,30},{8,0},{10,2},{12,4},{14,6},{16,8},{18,... | collective-permute-start | bytes 1179656 | tf_op jit(solution)/shard_map/ppermute | solution.py:185
  27.6 1.9 %collective-permute-start.2 = (bf16[1024,256]{1,0:T(8,128)(2,1)S(1)}, bf16[1024,256]{1,0:T(8,128)(2,1)S(1)}, u32[]{:S(2)}, u32[]{:S(2)}) collective-permute-start(bf16[1024,256]{1,0:T(8,128)(2,1)S(1)} %bitcast.3), channel_id=1, source_target_pairs={{0,8},{2,10},{4,12},{6,14},{8,16},{10,18},{12,20},{14,22},{16,24},... | collective-permute-start | bytes 1572872 | tf_op jit(solution)/shard_map/ppermute | solution.py:172
  29.5 6.9 %collective-permute-done = bf16[768,256]{1,0:T(8,128)(2,1)S(1)} collective-permute-done((bf16[768,256]{1,0:T(8,128)(2,1)S(1)}, bf16[768,256]{1,0:T(8,128)(2,1)S(1)}, u32[]{:S(2)}, u32[]{:S(2)}) %collective-permute-start) | collective-permute-done | bytes 393248 | tf_op jit(solution)/shard_map/ppermute | solution.py:185
  36.4 5.6 %collective-permute-start.1 = (bf16[768,256]{1,0:T(8,128)(2,1)S(1)}, bf16[768,256]{1,0:T(8,128)(2,1)S(1)}, u32[]{:S(2)}, u32[]{:S(2)}) collective-permute-start(bf16[768,256]{1,0:T(8,128)(2,1)S(1)} %collective-permute-done), channel_id=1, source_target_pairs={{24,16},{26,18},{28,20},{30,22},{0,24},{2,26},{4,28},{6,30},{8,32}... | collective-permute-start | bytes 1179656 | tf_op jit(solution)/shard_map/ppermute | solution.py:185
  42.0 3.4 %collective-permute-done.2.kv1_ref = bf16[1024,256]{1,0:T(8,128)(2,1)S(1)} collective-permute-done((bf16[1024,256]{1,0:T(8,128)(2,1)S(1)}, bf16[1024,256]{1,0:T(8,128)(2,1)S(1)}, u32[]{:S(2)}, u32[]{:S(2)}) %collective-permute-start.2) | collective-permute-done | bytes 524320 | tf_op jit(solution)/shard_map/ppermute | solution.py:172
  45.5 4.7 %collective-permute-done.1.kv2_ref = bf16[768,256]{1,0:T(8,128)(2,1)S(1)} collective-permute-done((bf16[768,256]{1,0:T(8,128)(2,1)S(1)}, bf16[768,256]{1,0:T(8,128)(2,1)S(1)}, u32[]{:S(2)}, u32[]{:S(2)}) %collective-permute-start.1) | collective-permute-done | bytes 393248 | tf_op jit(solution)/shard_map/ppermute | solution.py:185
  50.2 16.8 %attention.1 = (bf16[8,128,1024]{2,1,0:T(8,128)(2,1)}, bf16[768,256]{1,0:T(8,128)(2,1)S(1)}, bf16[1024,256]{1,0:T(8,128)(2,1)S(1)}, f32[1024,256]{1,0:T(8,128)S(1)}) custom-call(s32[16]{0:T(128)S(1)} %copy-done, bf16[8,128,1024]{2,1,0:T(8,128)(2,1)} %all-to-all-done.qg_ref, bf16[768,256]{1,0:T(8,128)(2,1)S(1)} %collective-permute-done.1.kv2_ref, ...), custom_call_target="tpu_custom_call" | custom-call | tf_op jit(solution)/shard_map/attention/pallas_call | solution.py:139
  67.0 4.4 %all-to-all-start.2 = ((bf16[8,128,1024]{2,1,0:T(8,128)(2,1)}), bf16[8,128,1024]{2,1,0:T(8,128)(2,1)}, u32[]{:S(2)}, u32[]{:S(2)}) async-start(bf16[8,128,1024]{2,1,0:T(8,128)(2,1)} %get-tuple-element.17), calls=%async_computation.2 | async-start | bytes 4194304 | tf_op jit(solution)/shard_map/all_to_all | solution.py:190
  71.4 9.3 %collective-permute-start.4 = (bf16[768,256]{1,0:T(8,128)(2,1)S(1)}, bf16[768,256]{1,0:T(8,128)(2,1)S(1)}, u32[]{:S(2)}, u32[]{:S(2)}) collective-permute-start(bf16[768,256]{1,0:T(8,128)(2,1)S(1)} %get-tuple-element.16), channel_id=1, source_target_pairs={{16,24},{18,26},{20,28},{22,30},{24,0},{26,2},{28,4},{30,6},{32,8}... | collective-permute-start | bytes 1179656 | tf_op jit(solution)/shard_map/ppermute | solution.py:185
  80.7 3.6 %collective-permute-start.3 = (bf16[1024,256]{1,0:T(8,128)(2,1)S(1)}, bf16[1024,256]{1,0:T(8,128)(2,1)S(1)}, u32[]{:S(2)}, u32[]{:S(2)}) collective-permute-start(bf16[1024,256]{1,0:T(8,128)(2,1)S(1)} %get-tuple-element.15), channel_id=1, source_target_pairs={{8,0},{10,2},{12,4},{14,6},{16,8},{18,10},{20,12},{22,14},{24,16},... | collective-permute-start | bytes 1572872 | tf_op jit(solution)/shard_map/ppermute | solution.py:172
  84.3 12.5 %collective-permute-done.4 = bf16[768,256]{1,0:T(8,128)(2,1)S(1)} collective-permute-done((bf16[768,256]{1,0:T(8,128)(2,1)S(1)}, bf16[768,256]{1,0:T(8,128)(2,1)S(1)}, u32[]{:S(2)}, u32[]{:S(2)}) %collective-permute-start.4) | collective-permute-done | bytes 393248 | tf_op jit(solution)/shard_map/ppermute | solution.py:185
  96.8 2.6 %collective-permute-start.5 = (bf16[768,256]{1,0:T(8,128)(2,1)S(1)}, bf16[768,256]{1,0:T(8,128)(2,1)S(1)}, u32[]{:S(2)}, u32[]{:S(2)}) collective-permute-start(bf16[768,256]{1,0:T(8,128)(2,1)S(1)} %collective-permute-done.4), channel_id=1, source_target_pairs={{24,0},{26,2},{28,4},{30,6},{0,8},{2,10},{4,12},{6,14},{8,16},{10,... | collective-permute-start | bytes 1179656 | tf_op jit(solution)/shard_map/ppermute | solution.py:185
  99.4 1.4 %collective-permute-done.3 = bf16[1024,256]{1,0:T(8,128)(2,1)S(1)} collective-permute-done((bf16[1024,256]{1,0:T(8,128)(2,1)S(1)}, bf16[1024,256]{1,0:T(8,128)(2,1)S(1)}, u32[]{:S(2)}, u32[]{:S(2)}) %collective-permute-start.3) | collective-permute-done | bytes 524320 | tf_op jit(solution)/shard_map/ppermute | solution.py:172
  100.8 10.0 %collective-permute-done.5 = bf16[768,256]{1,0:T(8,128)(2,1)S(1)} collective-permute-done((bf16[768,256]{1,0:T(8,128)(2,1)S(1)}, bf16[768,256]{1,0:T(8,128)(2,1)S(1)}, u32[]{:S(2)}, u32[]{:S(2)}) %collective-permute-start.5) | collective-permute-done | bytes 393248 | tf_op jit(solution)/shard_map/ppermute | solution.py:185
  110.8 0.9 add_convert_fusion
  111.8 4.2 %all-to-all-start.3 = ((bf16[8,128,256]{2,1,0:T(8,128)(2,1)}), bf16[8,128,256]{2,1,0:T(8,128)(2,1)S(1)}, u32[]{:S(2)}, u32[]{:S(2)}) async-start(bf16[8,128,256]{2,1,0:T(8,128)(2,1)} %bitcast.2), calls=%async_computation.3 | async-start | bytes 1048576 | tf_op jit(solution)/shard_map/all_to_all | solution.py:190
  116.0 3.8 %unpack.2 = (bf16[128,4096]{1,0:T(8,128)(2,1)}, bf16[128,4096]{1,0:T(8,128)(2,1)}) custom-call(bf16[8,128,1024]{2,1,0:T(8,128)(2,1)} %all-to-all-done.2.x_ref), custom_call_target="tpu_custom_call" | custom-call | tf_op jit(solution)/shard_map/unpack/pallas_call | solution.py:224
  119.8 6.6 %all-to-all-done.3.x_ref = bf16[8,128,256]{2,1,0:T(8,128)(2,1)S(1)} async-done(((bf16[8,128,256]{2,1,0:T(8,128)(2,1)}), bf16[8,128,256]{2,1,0:T(8,128)(2,1)S(1)}, u32[]{:S(2)}, u32[]{:S(2)}) %all-to-all-start.3) | async-done | bytes 524320 | tf_op jit(solution)/shard_map/all_to_all | solution.py:190
  126.3 0.9 unpack.3
  (5 shorter events, 0.0 us)
Async XLA Ops:
  2.5 15.7 %all-to-all-start.1 = ((bf16[8,128,256]{2,1,0:T(8,128)(2,1)}), bf16[8,128,256]{2,1,0:T(8,128)(2,1)S(1)}, u32[]{:S(2)}, u32[]{:S(2)}) async-start(bf16[8,128,256]{2,1,0:T(8,128)(2,1)} %pack.3), calls=%async_computation.1 | async-start | bytes 1048576 | tf_op jit(solution)/shard_map/all_to_all | solution.py:190
  11.6 38.6 %copy-start = (s32[16]{0:T(128)S(1)}, s32[16]{0:T(128)}, u32[]{:S(2)}) copy-start(s32[16]{0:T(128)} %doc_ref.1) | copy-start | bytes 196
  18.2 32.0 %all-to-all-start = ((bf16[8,128,1024]{2,1,0:T(8,128)(2,1)}), bf16[8,128,1024]{2,1,0:T(8,128)(2,1)}, u32[]{:S(2)}, u32[]{:S(2)}) async-start(bf16[8,128,1024]{2,1,0:T(8,128)(2,1)} %pack.2), calls=%async_computation | async-start | bytes 4194304 | tf_op jit(solution)/shard_map/all_to_all | solution.py:190
  22.6 13.8 %collective-permute-start = (bf16[768,256]{1,0:T(8,128)(2,1)S(1)}, bf16[768,256]{1,0:T(8,128)(2,1)S(1)}, u32[]{:S(2)}, u32[]{:S(2)}) collective-permute-start(bf16[768,256]{1,0:T(8,128)(2,1)S(1)} %bitcast.5), channel_id=1, source_target_pairs={{0,24},{2,26},{4,28},{6,30},{8,0},{10,2},{12,4},{14,6},{16,8},{18,... | collective-permute-start | bytes 1179656 | tf_op jit(solution)/shard_map/ppermute | solution.py:185
  27.6 17.9 %collective-permute-start.2 = (bf16[1024,256]{1,0:T(8,128)(2,1)S(1)}, bf16[1024,256]{1,0:T(8,128)(2,1)S(1)}, u32[]{:S(2)}, u32[]{:S(2)}) collective-permute-start(bf16[1024,256]{1,0:T(8,128)(2,1)S(1)} %bitcast.3), channel_id=1, source_target_pairs={{0,8},{2,10},{4,12},{6,14},{8,16},{10,18},{12,20},{14,22},{16,24},... | collective-permute-start | bytes 1572872 | tf_op jit(solution)/shard_map/ppermute | solution.py:172
  36.4 13.8 %collective-permute-start.1 = (bf16[768,256]{1,0:T(8,128)(2,1)S(1)}, bf16[768,256]{1,0:T(8,128)(2,1)S(1)}, u32[]{:S(2)}, u32[]{:S(2)}) collective-permute-start(bf16[768,256]{1,0:T(8,128)(2,1)S(1)} %collective-permute-done), channel_id=1, source_target_pairs={{24,16},{26,18},{28,20},{30,22},{0,24},{2,26},{4,28},{6,30},{8,32}... | collective-permute-start | bytes 1179656 | tf_op jit(solution)/shard_map/ppermute | solution.py:185
  67.0 44.8 %all-to-all-start.2 = ((bf16[8,128,1024]{2,1,0:T(8,128)(2,1)}), bf16[8,128,1024]{2,1,0:T(8,128)(2,1)}, u32[]{:S(2)}, u32[]{:S(2)}) async-start(bf16[8,128,1024]{2,1,0:T(8,128)(2,1)} %get-tuple-element.17), calls=%async_computation.2 | async-start | bytes 4194304 | tf_op jit(solution)/shard_map/all_to_all | solution.py:190
  71.4 25.4 %collective-permute-start.4 = (bf16[768,256]{1,0:T(8,128)(2,1)S(1)}, bf16[768,256]{1,0:T(8,128)(2,1)S(1)}, u32[]{:S(2)}, u32[]{:S(2)}) collective-permute-start(bf16[768,256]{1,0:T(8,128)(2,1)S(1)} %get-tuple-element.16), channel_id=1, source_target_pairs={{16,24},{18,26},{20,28},{22,30},{24,0},{26,2},{28,4},{30,6},{32,8}... | collective-permute-start | bytes 1179656 | tf_op jit(solution)/shard_map/ppermute | solution.py:185
  80.7 20.1 %collective-permute-start.3 = (bf16[1024,256]{1,0:T(8,128)(2,1)S(1)}, bf16[1024,256]{1,0:T(8,128)(2,1)S(1)}, u32[]{:S(2)}, u32[]{:S(2)}) collective-permute-start(bf16[1024,256]{1,0:T(8,128)(2,1)S(1)} %get-tuple-element.15), channel_id=1, source_target_pairs={{8,0},{10,2},{12,4},{14,6},{16,8},{18,10},{20,12},{22,14},{24,16},... | collective-permute-start | bytes 1572872 | tf_op jit(solution)/shard_map/ppermute | solution.py:172
  96.8 14.0 %collective-permute-start.5 = (bf16[768,256]{1,0:T(8,128)(2,1)S(1)}, bf16[768,256]{1,0:T(8,128)(2,1)S(1)}, u32[]{:S(2)}, u32[]{:S(2)}) collective-permute-start(bf16[768,256]{1,0:T(8,128)(2,1)S(1)} %collective-permute-done.4), channel_id=1, source_target_pairs={{24,0},{26,2},{28,4},{30,6},{0,8},{2,10},{4,12},{6,14},{8,16},{10,... | collective-permute-start | bytes 1179656 | tf_op jit(solution)/shard_map/ppermute | solution.py:185
  111.8 14.6 %all-to-all-start.3 = ((bf16[8,128,256]{2,1,0:T(8,128)(2,1)}), bf16[8,128,256]{2,1,0:T(8,128)(2,1)S(1)}, u32[]{:S(2)}, u32[]{:S(2)}) async-start(bf16[8,128,256]{2,1,0:T(8,128)(2,1)} %bitcast.2), calls=%async_computation.3 | async-start | bytes 1048576 | tf_op jit(solution)/shard_map/all_to_all | solution.py:190

commit v2 on v1

--- a/solution.py
+++ b/solution.py
@@ -8,7 +8,7 @@
 HEAD = 128
 GROUP = 4
 BLOCK = 256
-STEP = 1024
+STEP = 1536
 ROW = 1024
 BEHIND = 1792
 WINDOW = BEHIND + ROW

time: 127 us -> 127 us (level)
  starting transfers between devices: 46.2 us -> 43.6 us
  Pallas kernels: 27.2 us -> 29 us
    ppermute x2, waiting for transfers between devices: 4.86 us -> 12.2 us  [shift(): return lax.ppermute(x, ('x', 'y', 'z'), pairs)]
    ppermute x4, waiting for transfers between devices: 34.2 us -> 27.4 us  [shift_two(): x = lax.ppermute(x, ('x', 'y', 'z'), pairs)]
    pallas_call x1, Pallas kernels: 16.8 us -> 18.6 us  [attention(): pl.pallas_call(attention_kernel, grid=(TILES,), in_specs=[pl.BlockSpec(me...]
    ppermute x2, starting transfers between devices: 5.55 us -> 4.04 us  [shift(): return lax.ppermute(x, ('x', 'y', 'z'), pairs)]
where the time goes in v2:
time: 127 us
  waiting for transfers between devices  52.7 us (41%)
  starting transfers between devices  43.6 us (34%)
  Pallas kernels  29 us (23%)
    ppermute x4, waiting for transfers between devices, shift_two(): x = lax.ppermute(x, ('x', 'y', 'z'), pairs)  27.4 us
    ppermute x4, starting transfers between devices, shift_two(): x = lax.ppermute(x, ('x', 'y', 'z'), pairs)  21.3 us
    pallas_call x1, Pallas kernels, attention(): pl.pallas_call(attention_kernel, grid=(TILES,), in_specs=[pl.BlockSpec(me...  18.6 us
    all_to_all x4, starting transfers between devices, swap(): return lax.all_to_all(x, ROWS, split_axis=0, concat_axis=0, tiled=False)  18.2 us
    all_to_all x4, waiting for transfers between devices, swap(): return lax.all_to_all(x, ROWS, split_axis=0, concat_axis=0, tiled=False)  13.1 us
    ppermute x2, waiting for transfers between devices, shift(): return lax.ppermute(x, ('x', 'y', 'z'), pairs)  12.2 us
    pallas_call x2, Pallas kernels, pack(): pl.pallas_call(pack_kernel, grid=(steps,), in_specs=[pl.BlockSpec((tokens...  5.7 us
    pallas_call x2, Pallas kernels, unpack(): pl.pallas_call(unpack_kernel, grid=(steps,), in_specs=[pl.BlockSpec((8 //...  4.71 us
  transfers between devices with their start and end apart: 10, of which 8 were waited for; matrix products, arithmetic and copies ran while one was open for 1% of the time, Pallas kernels for 6%

profile of v2, /device:TPU:2, one launch (start us, length us, event | category | flops | bytes accessed | tf_op | source)
XLA Modules:
  0.0 127.0 jit_solution(4070936173012139612)
XLA Ops:
  0.6 1.9 %pack.3 = bf16[8,128,256]{2,1,0:T(8,128)(2,1)} custom-call(bf16[128,1024]{1,0:T(8,128)(2,1)} %a_ref.3, bf16[128,1024]{1,0:T(8,128)(2,1)} %b_ref.3), custom_call_target="tpu_custom_call" | custom-call | tf_op jit(solution)/shard_map/pack/pallas_call | solution.py:203
  2.5 5.3 %all-to-all-start.1 = ((bf16[8,128,256]{2,1,0:T(8,128)(2,1)}), bf16[8,128,256]{2,1,0:T(8,128)(2,1)S(1)}, u32[]{:S(2)}, u32[]{:S(2)}) async-start(bf16[8,128,256]{2,1,0:T(8,128)(2,1)} %pack.3), calls=%async_computation.1 | async-start | bytes 1048576 | tf_op jit(solution)/shard_map/all_to_all | solution.py:190
  7.9 3.8 %pack.2 = bf16[8,128,1024]{2,1,0:T(8,128)(2,1)} custom-call(bf16[128,4096]{1,0:T(8,128)(2,1)} %a_ref.2, bf16[128,4096]{1,0:T(8,128)(2,1)} %b_ref.2), custom_call_target="tpu_custom_call" | custom-call | tf_op jit(solution)/shard_map/pack/pallas_call | solution.py:203
  11.6 6.6 %all-to-all-done.1 = bf16[8,128,256]{2,1,0:T(8,128)(2,1)S(1)} async-done(((bf16[8,128,256]{2,1,0:T(8,128)(2,1)}), bf16[8,128,256]{2,1,0:T(8,128)(2,1)S(1)}, u32[]{:S(2)}, u32[]{:S(2)}) %all-to-all-start.1) | async-done | bytes 524320 | tf_op jit(solution)/shard_map/all_to_all | solution.py:190
  18.2 4.4 %all-to-all-start = ((bf16[8,128,1024]{2,1,0:T(8,128)(2,1)}), bf16[8,128,1024]{2,1,0:T(8,128)(2,1)}, u32[]{:S(2)}, u32[]{:S(2)}) async-start(bf16[8,128,1024]{2,1,0:T(8,128)(2,1)} %pack.2), calls=%async_computation | async-start | bytes 4194304 | tf_op jit(solution)/shard_map/all_to_all | solution.py:190
  22.6 4.9 %collective-permute-start = (bf16[768,256]{1,0:T(8,128)(2,1)S(1)}, bf16[768,256]{1,0:T(8,128)(2,1)S(1)}, u32[]{:S(2)}, u32[]{:S(2)}) collective-permute-start(bf16[768,256]{1,0:T(8,128)(2,1)S(1)} %bitcast.5), channel_id=1, source_target_pairs={{0,24},{2,26},{4,28},{6,30},{8,0},{10,2},{12,4},{14,6},{16,8},{18,... | collective-permute-start | bytes 1179656 | tf_op jit(solution)/shard_map/ppermute | solution.py:185
  27.6 1.9 %collective-permute-start.2 = (bf16[1024,256]{1,0:T(8,128)(2,1)S(1)}, bf16[1024,256]{1,0:T(8,128)(2,1)S(1)}, u32[]{:S(2)}, u32[]{:S(2)}) collective-permute-start(bf16[1024,256]{1,0:T(8,128)(2,1)S(1)} %bitcast.3), channel_id=1, source_target_pairs={{0,8},{2,10},{4,12},{6,14},{8,16},{10,18},{12,20},{14,22},{16,24},... | collective-permute-start | bytes 1572872 | tf_op jit(solution)/shard_map/ppermute | solution.py:172
  29.5 6.9 %collective-permute-done = bf16[768,256]{1,0:T(8,128)(2,1)S(1)} collective-permute-done((bf16[768,256]{1,0:T(8,128)(2,1)S(1)}, bf16[768,256]{1,0:T(8,128)(2,1)S(1)}, u32[]{:S(2)}, u32[]{:S(2)}) %collective-permute-start) | collective-permute-done | bytes 393248 | tf_op jit(solution)/shard_map/ppermute | solution.py:185
  36.4 5.6 %collective-permute-start.1 = (bf16[768,256]{1,0:T(8,128)(2,1)S(1)}, bf16[768,256]{1,0:T(8,128)(2,1)S(1)}, u32[]{:S(2)}, u32[]{:S(2)}) collective-permute-start(bf16[768,256]{1,0:T(8,128)(2,1)S(1)} %collective-permute-done), channel_id=1, source_target_pairs={{24,16},{26,18},{28,20},{30,22},{0,24},{2,26},{4,28},{6,30},{8,32}... | collective-permute-start | bytes 1179656 | tf_op jit(solution)/shard_map/ppermute | solution.py:185
  42.0 3.4 %collective-permute-done.2.kv1_ref = bf16[1024,256]{1,0:T(8,128)(2,1)S(1)} collective-permute-done((bf16[1024,256]{1,0:T(8,128)(2,1)S(1)}, bf16[1024,256]{1,0:T(8,128)(2,1)S(1)}, u32[]{:S(2)}, u32[]{:S(2)}) %collective-permute-start.2) | collective-permute-done | bytes 524320 | tf_op jit(solution)/shard_map/ppermute | solution.py:172
  45.5 4.7 %collective-permute-done.1.kv2_ref = bf16[768,256]{1,0:T(8,128)(2,1)S(1)} collective-permute-done((bf16[768,256]{1,0:T(8,128)(2,1)S(1)}, bf16[768,256]{1,0:T(8,128)(2,1)S(1)}, u32[]{:S(2)}, u32[]{:S(2)}) %collective-permute-start.1) | collective-permute-done | bytes 393248 | tf_op jit(solution)/shard_map/ppermute | solution.py:185
  50.2 18.6 %attention.1 = (bf16[8,128,1024]{2,1,0:T(8,128)(2,1)}, bf16[768,256]{1,0:T(8,128)(2,1)S(1)}, bf16[1024,256]{1,0:T(8,128)(2,1)S(1)}, f32[1024,256]{1,0:T(8,128)S(1)}) custom-call(s32[16]{0:T(128)S(1)} %copy-done, bf16[8,128,1024]{2,1,0:T(8,128)(2,1)} %all-to-all-done.qg_ref, bf16[768,256]{1,0:T(8,128)(2,1)S(1)} %collective-permute-done.1.kv2_ref, ...), custom_call_target="tpu_custom_call" | custom-call | tf_op jit(solution)/shard_map/attention/pallas_call | solution.py:139
  68.8 4.4 %all-to-all-start.2 = ((bf16[8,128,1024]{2,1,0:T(8,128)(2,1)}), bf16[8,128,1024]{2,1,0:T(8,128)(2,1)}, u32[]{:S(2)}, u32[]{:S(2)}) async-start(bf16[8,128,1024]{2,1,0:T(8,128)(2,1)} %get-tuple-element.17), calls=%async_computation.2 | async-start | bytes 4194304 | tf_op jit(solution)/shard_map/all_to_all | solution.py:190
  73.1 8.9 %collective-permute-start.4 = (bf16[768,256]{1,0:T(8,128)(2,1)S(1)}, bf16[768,256]{1,0:T(8,128)(2,1)S(1)}, u32[]{:S(2)}, u32[]{:S(2)}) collective-permute-start(bf16[768,256]{1,0:T(8,128)(2,1)S(1)} %get-tuple-element.16), channel_id=1, source_target_pairs={{16,24},{18,26},{20,28},{22,30},{24,0},{26,2},{28,4},{30,6},{32,8}... | collective-permute-start | bytes 1179656 | tf_op jit(solution)/shard_map/ppermute | solution.py:185
  82.0 2.1 %collective-permute-start.3 = (bf16[1024,256]{1,0:T(8,128)(2,1)S(1)}, bf16[1024,256]{1,0:T(8,128)(2,1)S(1)}, u32[]{:S(2)}, u32[]{:S(2)}) collective-permute-start(bf16[1024,256]{1,0:T(8,128)(2,1)S(1)} %get-tuple-element.15), channel_id=1, source_target_pairs={{8,0},{10,2},{12,4},{14,6},{16,8},{18,10},{20,12},{22,14},{24,16},... | collective-permute-start | bytes 1572872 | tf_op jit(solution)/shard_map/ppermute | solution.py:172
  84.2 7.3 %collective-permute-done.4 = bf16[768,256]{1,0:T(8,128)(2,1)S(1)} collective-permute-done((bf16[768,256]{1,0:T(8,128)(2,1)S(1)}, bf16[768,256]{1,0:T(8,128)(2,1)S(1)}, u32[]{:S(2)}, u32[]{:S(2)}) %collective-permute-start.4) | collective-permute-done | bytes 393248 | tf_op jit(solution)/shard_map/ppermute | solution.py:185
  91.5 1.9 %collective-permute-start.5 = (bf16[768,256]{1,0:T(8,128)(2,1)S(1)}, bf16[768,256]{1,0:T(8,128)(2,1)S(1)}, u32[]{:S(2)}, u32[]{:S(2)}) collective-permute-start(bf16[768,256]{1,0:T(8,128)(2,1)S(1)} %collective-permute-done.4), channel_id=1, source_target_pairs={{24,0},{26,2},{28,4},{30,6},{0,8},{2,10},{4,12},{6,14},{8,16},{10,... | collective-permute-start | bytes 1179656 | tf_op jit(solution)/shard_map/ppermute | solution.py:185
  93.4 8.8 %collective-permute-done.3 = bf16[1024,256]{1,0:T(8,128)(2,1)S(1)} collective-permute-done((bf16[1024,256]{1,0:T(8,128)(2,1)S(1)}, bf16[1024,256]{1,0:T(8,128)(2,1)S(1)}, u32[]{:S(2)}, u32[]{:S(2)}) %collective-permute-start.3) | collective-permute-done | bytes 524320 | tf_op jit(solution)/shard_map/ppermute | solution.py:172
  102.1 8.4 %collective-permute-done.5 = bf16[768,256]{1,0:T(8,128)(2,1)S(1)} collective-permute-done((bf16[768,256]{1,0:T(8,128)(2,1)S(1)}, bf16[768,256]{1,0:T(8,128)(2,1)S(1)}, u32[]{:S(2)}, u32[]{:S(2)}) %collective-permute-start.5) | collective-permute-done | bytes 393248 | tf_op jit(solution)/shard_map/ppermute | solution.py:185
  110.5 0.9 add_convert_fusion
  111.5 4.2 %all-to-all-start.3 = ((bf16[8,128,256]{2,1,0:T(8,128)(2,1)}), bf16[8,128,256]{2,1,0:T(8,128)(2,1)S(1)}, u32[]{:S(2)}, u32[]{:S(2)}) async-start(bf16[8,128,256]{2,1,0:T(8,128)(2,1)} %bitcast.2), calls=%async_computation.3 | async-start | bytes 1048576 | tf_op jit(solution)/shard_map/all_to_all | solution.py:190
  115.7 3.8 %unpack.2 = (bf16[128,4096]{1,0:T(8,128)(2,1)}, bf16[128,4096]{1,0:T(8,128)(2,1)}) custom-call(bf16[8,128,1024]{2,1,0:T(8,128)(2,1)} %all-to-all-done.2.x_ref), custom_call_target="tpu_custom_call" | custom-call | tf_op jit(solution)/shard_map/unpack/pallas_call | solution.py:224
  119.5 6.6 %all-to-all-done.3.x_ref = bf16[8,128,256]{2,1,0:T(8,128)(2,1)S(1)} async-done(((bf16[8,128,256]{2,1,0:T(8,128)(2,1)}), bf16[8,128,256]{2,1,0:T(8,128)(2,1)S(1)}, u32[]{:S(2)}, u32[]{:S(2)}) %all-to-all-start.3) | async-done | bytes 524320 | tf_op jit(solution)/shard_map/all_to_all | solution.py:190
  126.1 0.9 unpack.3
  (5 shorter events, 0.0 us)
Async XLA Ops:
  2.5 15.7 %all-to-all-start.1 = ((bf16[8,128,256]{2,1,0:T(8,128)(2,1)}), bf16[8,128,256]{2,1,0:T(8,128)(2,1)S(1)}, u32[]{:S(2)}, u32[]{:S(2)}) async-start(bf16[8,128,256]{2,1,0:T(8,128)(2,1)} %pack.3), calls=%async_computation.1 | async-start | bytes 1048576 | tf_op jit(solution)/shard_map/all_to_all | solution.py:190
  11.6 38.6 %copy-start = (s32[16]{0:T(128)S(1)}, s32[16]{0:T(128)}, u32[]{:S(2)}) copy-start(s32[16]{0:T(128)} %doc_ref.1) | copy-start | bytes 196
  18.2 32.0 %all-to-all-start = ((bf16[8,128,1024]{2,1,0:T(8,128)(2,1)}), bf16[8,128,1024]{2,1,0:T(8,128)(2,1)}, u32[]{:S(2)}, u32[]{:S(2)}) async-start(bf16[8,128,1024]{2,1,0:T(8,128)(2,1)} %pack.2), calls=%async_computation | async-start | bytes 4194304 | tf_op jit(solution)/shard_map/all_to_all | solution.py:190
  22.6 13.8 %collective-permute-start = (bf16[768,256]{1,0:T(8,128)(2,1)S(1)}, bf16[768,256]{1,0:T(8,128)(2,1)S(1)}, u32[]{:S(2)}, u32[]{:S(2)}) collective-permute-start(bf16[768,256]{1,0:T(8,128)(2,1)S(1)} %bitcast.5), channel_id=1, source_target_pairs={{0,24},{2,26},{4,28},{6,30},{8,0},{10,2},{12,4},{14,6},{16,8},{18,... | collective-permute-start | bytes 1179656 | tf_op jit(solution)/shard_map/ppermute | solution.py:185
  27.6 17.9 %collective-permute-start.2 = (bf16[1024,256]{1,0:T(8,128)(2,1)S(1)}, bf16[1024,256]{1,0:T(8,128)(2,1)S(1)}, u32[]{:S(2)}, u32[]{:S(2)}) collective-permute-start(bf16[1024,256]{1,0:T(8,128)(2,1)S(1)} %bitcast.3), channel_id=1, source_target_pairs={{0,8},{2,10},{4,12},{6,14},{8,16},{10,18},{12,20},{14,22},{16,24},... | collective-permute-start | bytes 1572872 | tf_op jit(solution)/shard_map/ppermute | solution.py:172
  36.4 13.8 %collective-permute-start.1 = (bf16[768,256]{1,0:T(8,128)(2,1)S(1)}, bf16[768,256]{1,0:T(8,128)(2,1)S(1)}, u32[]{:S(2)}, u32[]{:S(2)}) collective-permute-start(bf16[768,256]{1,0:T(8,128)(2,1)S(1)} %collective-permute-done), channel_id=1, source_target_pairs={{24,16},{26,18},{28,20},{30,22},{0,24},{2,26},{4,28},{6,30},{8,32}... | collective-permute-start | bytes 1179656 | tf_op jit(solution)/shard_map/ppermute | solution.py:185
  68.8 42.7 %all-to-all-start.2 = ((bf16[8,128,1024]{2,1,0:T(8,128)(2,1)}), bf16[8,128,1024]{2,1,0:T(8,128)(2,1)}, u32[]{:S(2)}, u32[]{:S(2)}) async-start(bf16[8,128,1024]{2,1,0:T(8,128)(2,1)} %get-tuple-element.17), calls=%async_computation.2 | async-start | bytes 4194304 | tf_op jit(solution)/shard_map/all_to_all | solution.py:190
  73.1 18.3 %collective-permute-start.4 = (bf16[768,256]{1,0:T(8,128)(2,1)S(1)}, bf16[768,256]{1,0:T(8,128)(2,1)S(1)}, u32[]{:S(2)}, u32[]{:S(2)}) collective-permute-start(bf16[768,256]{1,0:T(8,128)(2,1)S(1)} %get-tuple-element.16), channel_id=1, source_target_pairs={{16,24},{18,26},{20,28},{22,30},{24,0},{26,2},{28,4},{30,6},{32,8}... | collective-permute-start | bytes 1179656 | tf_op jit(solution)/shard_map/ppermute | solution.py:185
  82.0 20.1 %collective-permute-start.3 = (bf16[1024,256]{1,0:T(8,128)(2,1)S(1)}, bf16[1024,256]{1,0:T(8,128)(2,1)S(1)}, u32[]{:S(2)}, u32[]{:S(2)}) collective-permute-start(bf16[1024,256]{1,0:T(8,128)(2,1)S(1)} %get-tuple-element.15), channel_id=1, source_target_pairs={{8,0},{10,2},{12,4},{14,6},{16,8},{18,10},{20,12},{22,14},{24,16},... | collective-permute-start | bytes 1572872 | tf_op jit(solution)/shard_map/ppermute | solution.py:172
  91.5 19.1 %collective-permute-start.5 = (bf16[768,256]{1,0:T(8,128)(2,1)S(1)}, bf16[768,256]{1,0:T(8,128)(2,1)S(1)}, u32[]{:S(2)}, u32[]{:S(2)}) collective-permute-start(bf16[768,256]{1,0:T(8,128)(2,1)S(1)} %collective-permute-done.4), channel_id=1, source_target_pairs={{24,0},{26,2},{28,4},{30,6},{0,8},{2,10},{4,12},{6,14},{8,16},{10,... | collective-permute-start | bytes 1179656 | tf_op jit(solution)/shard_map/ppermute | solution.py:185
  111.5 14.6 %all-to-all-start.3 = ((bf16[8,128,256]{2,1,0:T(8,128)(2,1)}), bf16[8,128,256]{2,1,0:T(8,128)(2,1)S(1)}, u32[]{:S(2)}, u32[]{:S(2)}) async-start(bf16[8,128,256]{2,1,0:T(8,128)(2,1)} %bitcast.2), calls=%async_computation.3 | async-start | bytes 1048576 | tf_op jit(solution)/shard_map/all_to_all | solution.py:190
